TPU v7x, 32 devices: a whole 2x2x4 slice. The times are simulated.
32 devices in a mesh: groups: 2 (over y), dp: 4 (over z), chan: 2 (over x), sub: 2 (over core).
Axes of the slice: x: 2, y: 2, z: 4, core: 2. Of those that a mesh axis runs over, the one named last changes fastest.
Arguments:
- features: bfloat16 [192, 128, 1536], P(('groups', 'dp', 'sub'), None, 'chan'), parts along dimension 0, may hold values from -6 to 6
- cotangent: bfloat16 [192, 128, 1536], P(('groups', 'dp', 'sub'), None, 'chan'), parts along dimension 0, may hold values from -0.076171875 to 0.076171875
- snake_alpha: float32 [1536], P('chan'), may hold values from 0.5 to 4
- conv_weight: bfloat16 [1536, 3, 1536], P('dp', None, 'chan'), may hold values from -0.09375 to 0.09375
- lengths: int32 [192], P(('groups', 'dp', 'sub')), parts along dimension 0, may hold values from 1 to 128, as said below
- kept_rows: int32 [16], P(('groups', 'dp', 'sub')), parts along dimension 0, may hold values from 1 to 6, as said below
- sent_rows: int32 [16], P(('groups', 'dp', 'sub')), parts along dimension 0, may hold values from 0 to 6, as said below
Outputs:
- balanced_out: bfloat16 [112, 128, 1536], P(('groups', 'dp', 'sub'), None, 'chan'), parts along dimension 0
- weight_grad: float32 [3072, 3, 1536], P(('groups', 'dp'), None, 'chan'), parts along dimension 0
There are 2 independent parts, one for each index of `groups`. A program takes and returns all parts, laid end to end along the dimension named above; an argument that names none is the same for every part. Nothing has to cross between parts.
Inputs may be any that keep to these rules, and one draw needn't show every extreme that they name: `kept_rows`: each device keeps at least one row; one device keeps 6. kept_rows[h] + sent_rows[p] <= 7 for every device h and its previous device p; some device hands on 6 rows and some none. The first slot of every device has length 128; lengths of empty slots are not read.
All inputs are finite; a program needn't handle non-finite values.
Results may differ from a plain program's by a relative error of at most 0.01.
Values may be sent and summed in bfloat16 or wider, within the bound.
A program may use at most 128 MiB of HBM per device.

v0:
```python
import jax
import jax.numpy as jnp
from jax import lax
from jax.sharding import PartitionSpec as P

KERNEL_TAPS = 3
DILATION_STEP = 3


def from_behind(value, axis, by):
    devices = lax.axis_size(axis)
    return lax.ppermute(value, axis, [(i, (i + by) % devices) for i in range(devices)])


def snake_rows(rows, snake_alpha, time_mask):
    values = rows.astype(jnp.float32)
    shaped = values + jnp.sin(snake_alpha * values) ** 2 / snake_alpha
    return (shaped * time_mask[:, :, None]).astype(jnp.bfloat16)


def on_device(features, cotangent, snake_alpha, conv_weight, lengths, kept_rows, sent_rows):
    slots_in = features.shape[0]
    keep_count = slots_in // 2
    capacity = keep_count + 1
    step_total = features.shape[1]
    chan_width = features.shape[2]
    own_keep = kept_rows[0]
    own_sent = sent_rows[0]
    move_slots = jnp.arange(keep_count)
    keep_slots = jnp.arange(keep_count)
    moved_feat = lax.dynamic_slice_in_dim(features, own_keep, keep_count, 0)
    moved_cot = lax.dynamic_slice_in_dim(cotangent, own_keep, keep_count, 0)
    moved_len = jnp.where(
        move_slots < own_sent, lax.dynamic_slice_in_dim(lengths, own_keep, keep_count, 0), 0
    ).astype(jnp.bfloat16)
    arrived_feat, arrived_cot, arrived_len = from_behind(
        (moved_feat, moved_cot, moved_len), "dp", 1
    )

    def place_rows(own_part, arrived):
        blank_rows = jnp.zeros((keep_count,) + own_part.shape[1:], own_part.dtype)
        buffer = jnp.concatenate([own_part, blank_rows], axis=0)
        buffer = lax.dynamic_update_slice_in_dim(buffer, arrived, own_keep, 0)
        return buffer[:capacity]

    own_len = jnp.where(keep_slots < own_keep, lengths[:keep_count], 0)
    rows_bal = place_rows(features[:keep_count], arrived_feat)
    cot_bal = place_rows(cotangent[:keep_count], arrived_cot)
    len_bal = place_rows(own_len, arrived_len.astype(jnp.int32))
    time_mask = (jnp.arange(step_total)[None, :] < len_bal[:, None]).astype(jnp.float32)
    local_act = snake_rows(rows_bal, snake_alpha, time_mask)
    complete_output = lax.all_gather(local_act, "chan", axis=2, tiled=True)
    padded_width = complete_output.shape[2]
    padded_input = jnp.pad(complete_output, ((0, 0), (DILATION_STEP, DILATION_STEP), (0, 0)))
    flattened_rows = capacity * step_total
    shifted_tap_rows = [
        padded_input[
            :, tap_number * DILATION_STEP : tap_number * DILATION_STEP + step_total, :
        ].reshape(flattened_rows, padded_width)
        for tap_number in range(KERNEL_TAPS)
    ]
    running = jnp.zeros((flattened_rows, chan_width), jnp.float32)
    panel_rows = lax.all_gather(conv_weight, "dp", axis=0, tiled=True)
    for tap_number in range(KERNEL_TAPS):
        columns = shifted_tap_rows[tap_number]
        running = running + jnp.dot(
            columns, panel_rows[:, tap_number, :], preferred_element_type=jnp.float32
        )
    result = (
        rows_bal.astype(jnp.float32) + running.reshape(capacity, step_total, chan_width)
    ) * time_mask[:, :, None]
    balanced_out = result.astype(jnp.bfloat16)
    cot_mask = jnp.where(time_mask[:, :, None] > 0.0, cot_bal, jnp.zeros_like(cot_bal)).reshape(
        flattened_rows, chan_width
    )
    products = []
    for tap_number in range(KERNEL_TAPS):
        columns = shifted_tap_rows[tap_number]
        products.append(
            lax.dot_general(
                columns, cot_mask, (((0,), (0,)), ((), ())), preferred_element_type=jnp.float32
            )
        )
    shard_sum = lax.psum_scatter(
        jnp.stack(products, axis=1).astype(jnp.bfloat16), "dp", scatter_dimension=0, tiled=True
    )
    weight_grad = lax.psum(shard_sum, "sub").astype(jnp.float32)
    return (balanced_out, weight_grad)


def solution(mesh):
    placed = (
        P(("groups", "dp", "sub"), None, "chan"),
        P(("groups", "dp", "sub"), None, "chan"),
        P("chan"),
        P("dp", None, "chan"),
        P(("groups", "dp", "sub")),
        P(("groups", "dp", "sub")),
        P(("groups", "dp", "sub")),
    )
    return jax.shard_map(
        on_device,
        mesh=mesh,
        in_specs=placed,
        out_specs=(P(("groups", "dp", "sub"), None, "chan"), P(("groups", "dp"), None, "chan")),
        check_vma=False,
    )
```

profile of v0, /device:TPU:0, one launch (start us, length us, event | category | flops | bytes accessed | tf_op | source)
XLA Modules:
  0.0 383.4 jit_solution(10857712576062909988)
XLA Ops:
  7.9 3.0 copy.18
  12.1 3.0 collective-permute-start
  17.5 3.0 copy.24
  20.6 3.5 broadcast_select_fusion
  24.0 19.4 %collective-permute-done.1 = bf16[6]{0:T(256)(128)(2,1)S(1)} collective-permute-done((bf16[6]{0:T(256)(128)(2,1)S(1)}, bf16[6]{0:T(256)(128)(2,1)S(1)}, u32[]{:S(2)}, u32[]{:S(2)}) %collective-permute-start.1) | collective-permute-done | bytes 44 | tf_op jit(solution)/shard_map/ppermute | solution.py:12
  45.2 10.8 %fusion.7 = bf16[7,128,768]{1,2,0:T(8,128)(2,1)} fusion(f32[7,128]{1,0:T(8,128)S(1)} %get-tuple-element.9, f32[768]{0:T(1024)S(1)} %copy-done.7, bf16[12,128,768]{1,2,0:T(8,128)(2,1)S(1)} %constant_dynamic-update-slice_fusion.1), kind=kLoop, calls=%fused_computation.16 | loop fusion | flops 4816896 | bytes 2759168 | tf_op jit(solution)/shard_map/convert_element_type | solution.py:18
  56.9 28.9 %collective-permute-done.2 = bf16[6,128,768]{1,2,0:T(8,128)(2,1)S(1)} collective-permute-done((bf16[6,128,768]{1,2,0:T(8,128)(2,1)S(1)}, bf16[6,128,768]{1,2,0:T(8,128)(2,1)S(1)}, u32[]{:S(2)}, u32[]{:S(2)}) %collective-permute-start.2) | collective-permute-done | bytes 1179680 | tf_op jit(solution)/shard_map/ppermute | solution.py:12
  86.9 9.1 %all-gather.3.cloned.1.call-done = bf16[7,128,1536]{1,2,0:T(8,128)(2,1)} async-done(((bf16[7,128,768]{1,2,0:T(8,128)(2,1)}), bf16[7,128,1536]{1,2,0:T(8,128)(2,1)}) %all-gather.3.cloned.1.call-update) | async-done | bytes 2752528 | tf_op jit(solution)/shard_map/all_gather | solution.py:52
  96.0 5.0 %fusion = bf16[1536,1,768]{2,0,1:T(8,128)(2,1)S(1)} fusion(bf16[12,128,768]{1,2,0:T(8,128)(2,1)} %constant_dynamic-update-slice_fusion, pred[7,128]{1,0:T(8,128)(4,1)S(1)} %get-tuple-element.8, bf16[7,128,1536]{1,2,0:T(8,128)(2,1)} %all-gather.3.cloned.1.call-done), kind=kOutput, calls=%fused_computation.9 | convolution fusion | flops 2115796992 | bytes 6488960 | tf_op jit(solution)/shard_map/dot_general | solution.py:80
  101.0 2.9 fusion.2
  103.9 2.9 fusion.1
  106.8 3.5 pad_maximum_fusion
  110.5 3.3 pad_slice_fusion.1
  113.8 4.6 %copy.22 = bf16[7,128,1536]{2,1,0:T(8,128)(2,1)} copy(bf16[7,128,1536]{1,2,0:T(8,128)(2,1)} %get-tuple-element.7) | data formatting | bytes 5505024 | tf_op jit(solution)/shard_map/slice | solution.py:57
  118.4 4.7 %copy.20 = bf16[7,128,1536]{2,1,0:T(8,128)(2,1)} copy(bf16[7,128,1536]{1,2,0:T(8,128)(2,1)} %get-tuple-element.6) | data formatting | bytes 5505024 | tf_op jit(solution)/shard_map/slice | solution.py:57
  126.0 99.9 %all-gather.5.cloned.1.call-done = bf16[1536,3,768]{2,0,1:T(8,128)(2,1)} async-done(((bf16[384,3,768]{2,0,1:T(8,128)(2,1)}), bf16[1536,3,768]{2,0,1:T(8,128)(2,1)}) %all-gather.5.cloned.1.call-update) | async-done | bytes 7077904 | tf_op jit(solution)/shard_map/all_gather | solution.py:63
  225.8 6.5 %fusion.10 = f32[896,768]{1,0:T(8,128)} fusion(bf16[896,1536]{1,0:T(8,128)(2,1)} %bitcast.47, bf16[1536,3,768]{2,0,1:T(8,128)(2,1)} %all-gather.5.cloned.1.call-done), kind=kOutput, calls=%fused_computation.21 | convolution fusion | flops 2113929216 | bytes 7864320 | tf_op jit(solution)/shard_map/dot_general | solution.py:66
  232.3 117.5 %reduce-scatter.2.cloned.1.call-done = bf16[384,3,768]{2,0,1:T(8,128)(2,1)} async-done(((bf16[1536,3,768]{2,0,1:T(8,128)(2,1)}), bf16[384,3,768]{2,0,1:T(8,128)(2,1)}) %reduce-scatter.2.cloned.1.call-update) | async-done | bytes 1769488 | tf_op jit(solution)/shard_map/reduce_scatter | solution.py:84
  349.9 4.1 %fusion.11 = f32[896,768]{1,0:T(8,128)S(1)} fusion(bf16[896,1536]{1,0:T(8,128)(2,1)S(1)} %bitcast.46, bf16[1536,3,768]{2,0,1:T(8,128)(2,1)} %all-gather.5.cloned.1.call-done), kind=kOutput, calls=%fused_computation.23 | convolution fusion | flops 2113929216 | bytes 7864320 | tf_op jit(solution)/shard_map/dot_general | solution.py:66
  354.0 5.5 %add_add_fusion = f32[896,768]{1,0:T(8,128)} fusion(f32[896,768]{1,0:T(8,128)S(1)} %copy-done.10, f32[896,768]{1,0:T(8,128)S(1)} %fusion.11, bf16[896,1536]{1,0:T(8,128)(2,1)S(1)} %bitcast.45, bf16[1536,3,768]{2,0,1:T(8,128)(2,1)} %all-gather.5.cloned.1.call-done), kind=kOutput, calls=%fused_computation.19 | convolution fusion | flops 2115305472 | bytes 13369344 | tf_op jit(solution)/shard_map/dot_general | solution.py:66
  359.5 3.6 copy.23
  363.1 3.2 fusion.9
  368.8 4.5 %all-reduce.4.cloned.1.call-done = bf16[384,3,768]{2,0,1:T(8,128)(2,1)} async-done(((bf16[384,3,768]{2,0,1:T(8,128)(2,1)}), bf16[384,3,768]{2,0,1:T(8,128)(2,1)}) %all-reduce.4.cloned.1.call-update) | async-done | bytes 1769488 | tf_op jit(solution)/shard_map/psum | solution.py:87
  373.3 3.6 convert_element_type.38
  (43 shorter events, 12.3 us)
Async XLA Ops:
  7.2 88.8 %all-gather.3.cloned.1.call-start = ((), (), s32[]{:S(2)}) async-start(), calls=%async_computation.1 | async-start | bytes 4128768 | tf_op jit(solution)/shard_map/all_gather | solution.py:52
  7.9 8.0 %copy-start.8 = (s32[12]{0:T(128)S(1)}, s32[12]{0:T(128)}, u32[]{:S(2)}) copy-start(s32[12]{0:T(128)} %param.11) | copy-start | bytes 148
  10.9 6.6 %copy-start = (bf16[12,128,768]{1,2,0:T(8,128)(2,1)}, bf16[12,128,768]{1,2,0:T(8,128)(2,1)S(1)}, u32[]{:S(2)}) copy-start(bf16[12,128,768]{1,2,0:T(8,128)(2,1)S(1)} %copy.18) | copy-start | bytes 7077892
  12.1 8.4 %copy-start.9 = (pred[12]{0:T(512)(128)(4,1)S(1)}, pred[12]{0:T(512)(128)(4,1)}, u32[]{:S(2)}) copy-start(pred[12]{0:T(512)(128)(4,1)} %constant.5.clone.1) | copy-start | bytes 40
  12.1 31.5 %collective-permute-start = (bf16[6,128,768]{1,2,0:T(8,128)(2,1)}, bf16[6,128,768]{1,2,0:T(8,128)(2,1)S(1)}, u32[]{:S(2)}, u32[]{:S(2)}) collective-permute-start(bf16[6,128,768]{1,2,0:T(8,128)(2,1)} %constant_dynamic-slice_fusion.1), channel_id=1, source_target_pairs={{0,4},{4,8},{8,12},{12,0},{1,5},{5,9},{9,13},{13,1},{2,6},{6,10},{... | collective-permute-start | bytes 3538952 | tf_op jit(solution)/shard_map/ppermute | solution.py:12
  15.9 27.5 %collective-permute-start.1 = (bf16[6]{0:T(256)(128)(2,1)S(1)}, bf16[6]{0:T(256)(128)(2,1)S(1)}, u32[]{:S(2)}, u32[]{:S(2)}) collective-permute-start(bf16[6]{0:T(256)(128)(2,1)S(1)} %get-tuple-element.12), channel_id=1, source_target_pairs={{0,4},{4,8},{8,12},{12,0},{1,5},{5,9},{9,13},{13,1},{2,6},{6,10},{... | collective-permute-start | bytes 44 | tf_op jit(solution)/shard_map/ppermute | solution.py:12
  20.5 24.6 %copy-start.7 = (f32[768]{0:T(1024)S(1)}, f32[768]{0:T(1024)}, u32[]{:S(2)}) copy-start(f32[768]{0:T(1024)} %param.9) | copy-start | bytes 9220
  43.8 1.4 copy-start.1
  56.0 169.9 %all-gather.5.cloned.1.call-start = ((), (), s32[]{:S(2)}) async-start(), calls=%async_computation.2 | async-start | bytes 8847360 | tf_op jit(solution)/shard_map/all_gather | solution.py:63
  56.7 293.1 %reduce-scatter.2.cloned.1.call-start = ((), (), s32[]{:S(2)}) async-start(), calls=%async_computation.3 | async-start | bytes 8847360 | tf_op jit(solution)/shard_map/reduce_scatter | solution.py:84
  56.8 28.9 %collective-permute-start.2 = (bf16[6,128,768]{1,2,0:T(8,128)(2,1)S(1)}, bf16[6,128,768]{1,2,0:T(8,128)(2,1)S(1)}, u32[]{:S(2)}, u32[]{:S(2)}) collective-permute-start(bf16[6,128,768]{1,2,0:T(8,128)(2,1)S(1)} %constant_dynamic-slice_fusion), channel_id=1, source_target_pairs={{0,4},{4,8},{8,12},{12,0},{1,5},{5,9},{9,13},{13,1},{2,6},{6,10},{... | collective-permute-start | bytes 3538952 | tf_op jit(solution)/shard_map/ppermute | solution.py:12
  96.0 5.0 %copy-start.3 = (bf16[7,128,1536]{1,2,0:T(8,128)(2,1)S(1)}, bf16[7,128,1536]{1,2,0:T(8,128)(2,1)}, u32[]{:S(2)}) copy-start(bf16[7,128,1536]{1,2,0:T(8,128)(2,1)} %all-gather.3.cloned.1.call-done) | copy-start | bytes 8257540
  96.0 5.0 %copy-start.6 = (bf16[12,128,768]{1,2,0:T(8,128)(2,1)S(1)}, bf16[12,128,768]{1,2,0:T(8,128)(2,1)}, u32[]{:S(2)}) copy-start(bf16[12,128,768]{1,2,0:T(8,128)(2,1)} %constant_dynamic-update-slice_fusion) | copy-start | bytes 7077892
  110.3 263.0 %all-reduce.4.cloned.1.call-start = ((), (), s32[]{:S(2)}) async-start(), calls=%async_computation.4 | async-start | bytes 3538944 | tf_op jit(solution)/shard_map/psum | solution.py:87
  225.8 124.0 %copy-start.5 = (bf16[7,128,1536]{2,1,0:T(8,128)(2,1)S(1)}, bf16[7,128,1536]{2,1,0:T(8,128)(2,1)}, u32[]{:S(2)}) copy-start(bf16[7,128,1536]{2,1,0:T(8,128)(2,1)} %copy.21) | copy-start | bytes 8257540
  349.9 4.1 %copy-start.4 = (bf16[7,128,1536]{2,1,0:T(8,128)(2,1)S(1)}, bf16[7,128,1536]{2,1,0:T(8,128)(2,1)}, u32[]{:S(2)}) copy-start(bf16[7,128,1536]{2,1,0:T(8,128)(2,1)} %copy.20) | copy-start | bytes 8257540
  349.9 4.1 %copy-start.10 = (f32[896,768]{1,0:T(8,128)S(1)}, f32[896,768]{1,0:T(8,128)}, u32[]{:S(2)}) copy-start(f32[896,768]{1,0:T(8,128)} %fusion.10) | copy-start | bytes 8257540
  359.5 3.6 copy-start.2
Sparse Core Ops, SparseCore 0:
  56.1 39.8 all-gather.2
  97.6 128.2 all-gather.4
  228.1 121.6 reduce-scatter.1
  352.0 21.2 all-reduce.3
where the time goes:
time: 384 us; the launch traced here: 383 us
  waiting for transfers between devices  280 us (73%)
  local copies, waits for them, and re-layouts  31.6 us (8%)
  matrix products  26.8 us (7%)
  other arithmetic  24.7 us (6%)
  between operations  15.3 us (4%)
  starting transfers between devices  5 us (1%)
    reduce_scatter x1, waiting for transfers between devices, on_device(): lax.psum_scatter(jnp.stack(products, axis=1).astype(jnp.bfloat16), 'dp',...  118 us
    all_gather x1, waiting for transfers between devices, on_device(): panel_rows = lax.all_gather(conv_weight, 'dp', axis=0, tiled=True)  99.9 us
    ppermute x3, waiting for transfers between devices, from_behind(): lax.ppermute(value, axis, [(i, (i + by) % devices) for i in range(devices)])  48.3 us
    dot_general x3, matrix products, on_device(): jnp.dot(columns, panel_rows[:, tap_number, :], preferred_element_type=jnp...  16.1 us
    slice x3, local copies, waits for them, and re-layouts, on_device(): padded_input[:, tap_number * DILATION_STEP:tap_number * DILATION_STEP + s...  12.6 us
    dot_general x3, matrix products, on_device(): lax.dot_general(columns, cot_mask, (((0,), (0,)), ((), ())), preferred_el...  10.8 us
    convert_element_type x1, other arithmetic, snake_rows(): return (shaped * time_mask[:, :, None]).astype(jnp.bfloat16)  10.8 us
    unnamed x25, local copies, waits for them, and re-layouts  10 us
  transfers between devices with their start and end apart: 7, of which 6 were waited for; matrix products, arithmetic and copies ran while one was open for 16% of the time, Pallas kernels for 0%

commit v1 on v0

--- a/solution.py
+++ b/solution.py
@@ -49,7 +49,15 @@
     len_bal = place_rows(own_len, arrived_len.astype(jnp.int32))
     time_mask = (jnp.arange(step_total)[None, :] < len_bal[:, None]).astype(jnp.float32)
     local_act = snake_rows(rows_bal, snake_alpha, time_mask)
-    complete_output = lax.all_gather(local_act, "chan", axis=2, tiled=True)
+    ways, here, turn = (lax.axis_size("chan"), lax.axis_index("chan"), local_act.shape[2])
+    line, have = (local_act, 1)
+    while have < ways:
+        line = jnp.concatenate(
+            [line, lax.ppermute(line, "chan", [(d, (d - have) % ways) for d in range(ways)])],
+            axis=2,
+        )
+        have = 2 * have
+    complete_output = jnp.roll(line, here * turn, axis=2)
     padded_width = complete_output.shape[2]
     padded_input = jnp.pad(complete_output, ((0, 0), (DILATION_STEP, DILATION_STEP), (0, 0)))
     flattened_rows = capacity * step_total

time: 384 us -> 355 us (0.924)
  waiting for transfers between devices: 280 us -> 224 us
  starting transfers between devices: 5 us -> 29.4 us
  other arithmetic: 24.7 us -> 29.5 us
    all_gather x1, waiting for transfers between devices: 99.9 us -> 2.74 us  [on_device(): panel_rows = lax.all_gather(conv_weight, 'dp', axis=0, tiled=True)]
    ppermute x3, waiting for transfers between devices: 48.3 us -> 85.9 us  [from_behind(): lax.ppermute(value, axis, [(i, (i + by) % devices) for i in range(devices)])]
    ppermute x3, starting transfers between devices: 4.66 us -> 27.3 us  [from_behind(): lax.ppermute(value, axis, [(i, (i + by) % devices) for i in range(devices)])]
    reduce_scatter x1, waiting for transfers between devices: 118 us -> 130 us  [on_device(): lax.psum_scatter(jnp.stack(products, axis=1).astype(jnp.bfloat16), 'dp',...]
    all_gather x1 -> x0, waiting for transfers between devices: 9.13 us -> none  [on_device(): complete_output = lax.all_gather(local_act, 'chan', axis=2, tiled=True)]
    concatenate x0 -> x1, other arithmetic: none -> 5.21 us  [on_device(): complete_output = jnp.roll(line, here * turn, axis=2)]
    unnamed x25 -> x27, local copies, waits for them, and re-layouts: 10 us -> 10.1 us
  transfers between devices with their start and end apart: 7 -> 7, of which waited for: 6 -> 5; matrix products, arithmetic and copies ran while one was open for 16% -> 23% of each run, Pallas kernels for 0% -> 0%
where the time goes in v1:
time: 355 us; the launch traced here: 354 us
  waiting for transfers between devices  224 us (63%)
  local copies, waits for them, and re-layouts  30.9 us (9%)
  other arithmetic  29.5 us (8%)
  starting transfers between devices  29.4 us (8%)
  matrix products  24.8 us (7%)
  between operations  15.2 us (4%)
    reduce_scatter x1, waiting for transfers between devices, on_device(): lax.psum_scatter(jnp.stack(products, axis=1).astype(jnp.bfloat16), 'dp',...  130 us
    ppermute x3, waiting for transfers between devices, from_behind(): lax.ppermute(value, axis, [(i, (i + by) % devices) for i in range(devices)])  85.9 us
    ppermute x3, starting transfers between devices, from_behind(): lax.ppermute(value, axis, [(i, (i + by) % devices) for i in range(devices)])  27.3 us
    dot_general x3, matrix products, on_device(): jnp.dot(columns, panel_rows[:, tap_number, :], preferred_element_type=jnp...  16.1 us
    slice x3, local copies, waits for them, and re-layouts, on_device(): padded_input[:, tap_number * DILATION_STEP:tap_number * DILATION_STEP + s...  10.9 us
    convert_element_type x1, other arithmetic, snake_rows(): return (shaped * time_mask[:, :, None]).astype(jnp.bfloat16)  10.1 us
    unnamed x27, local copies, waits for them, and re-layouts  10.1 us
    dot_general x3, matrix products, on_device(): lax.dot_general(columns, cot_mask, (((0,), (0,)), ((), ())), preferred_el...  8.71 us
  transfers between devices with their start and end apart: 7, of which 5 were waited for; matrix products, arithmetic and copies ran while one was open for 23% of the time, Pallas kernels for 0%

profile of v1, /device:TPU:0, one launch (start us, length us, event | category | flops | bytes accessed | tf_op | source)
XLA Modules:
  0.0 354.4 jit_solution(1191575255116587250)
XLA Ops:
  8.6 3.0 copy.18
  12.8 3.0 collective-permute-start
  18.1 4.5 %copy.24 = bf16[12,128,768]{1,2,0:T(8,128)(2,1)} copy(bf16[12,128,768]{2,1,0:T(8,128)(2,1)} %param.8) | data formatting | bytes 4718592 | tf_op args[1]
  22.6 3.8 %broadcast_select_fusion = (bf16[12,128,768]{1,2,0:T(8,128)(2,1)}, bf16[12,128,768]{1,2,0:T(8,128)(2,1)S(1)}) fusion(bf16[12,128,768]{1,2,0:T(8,128)(2,1)} %copy.24, pred[12]{0:T(512)(128)(4,1)S(1)} %copy-done.10, bf16[12,128,768]{1,2,0:T(8,128)(2,1)S(1)} %copy.18), kind=kLoop, calls=%fused_computation.33 | loop fusion | flops 2359296 | bytes 9437196 | tf_op jit(solution)/shard_map/concatenate | solution.py:42
  26.4 36.6 %collective-permute-done.1 = bf16[6]{0:T(256)(128)(2,1)S(1)} collective-permute-done((bf16[6]{0:T(256)(128)(2,1)S(1)}, bf16[6]{0:T(256)(128)(2,1)S(1)}, u32[]{:S(2)}, u32[]{:S(2)}) %collective-permute-start.1) | collective-permute-done | bytes 44 | tf_op jit(solution)/shard_map/ppermute | solution.py:12
  63.3 10.1 %fusion.7 = bf16[7,128,768]{1,2,0:T(8,128)(2,1)S(1)} fusion(f32[7,128]{1,0:T(8,128)S(1)} %get-tuple-element.9, f32[768]{0:T(1024)S(1)} %copy-done.8, bf16[12,128,768]{1,2,0:T(8,128)(2,1)S(1)} %constant_dynamic-update-slice_fusion.1), kind=kLoop, calls=%fused_computation.20 | loop fusion | flops 4816896 | bytes 2759168 | tf_op jit(solution)/shard_map/convert_element_type | solution.py:18
  76.3 22.7 %collective-permute-start.3 = (bf16[6,128,768]{1,2,0:T(8,128)(2,1)}, bf16[6,128,768]{1,2,0:T(8,128)(2,1)S(1)}, u32[]{:S(2)}, u32[]{:S(2)}) collective-permute-start(bf16[6,128,768]{1,2,0:T(8,128)(2,1)} %constant_dynamic-slice_fusion), channel_id=1, source_target_pairs={{0,4},{4,8},{8,12},{12,0},{1,5},{5,9},{9,13},{13,1},{2,6},{6,10},{... | collective-permute-start | bytes 3538952 | tf_op jit(solution)/shard_map/ppermute | solution.py:12
  99.0 49.3 %collective-permute-done.3 = bf16[6,128,768]{1,2,0:T(8,128)(2,1)S(1)} collective-permute-done((bf16[6,128,768]{1,2,0:T(8,128)(2,1)}, bf16[6,128,768]{1,2,0:T(8,128)(2,1)S(1)}, u32[]{:S(2)}, u32[]{:S(2)}) %collective-permute-start.3) | collective-permute-done | bytes 1179680 | tf_op jit(solution)/shard_map/ppermute | solution.py:12
  149.5 5.2 %fusion.12 = bf16[7,128,1536]{1,2,0:T(8,128)(2,1)S(1)} fusion(s32[]{:T(128)S(6)} %select_n.36, bf16[7,128,768]{1,2,0:T(8,128)(2,1)} %copy-done.4, bf16[7,128,768]{1,2,0:T(8,128)(2,1)} %collective-permute-done.2), kind=kLoop, calls=%fused_computation.25 | loop fusion | flops 11010048 | bytes 5505028 | tf_op jit(solution)/shard_map/jit(_roll_dynamic)/concatenate | solution.py:60
  154.8 2.9 fusion
  157.7 2.9 fusion.2
  160.6 2.9 fusion.1
  163.5 3.4 pad_maximum_fusion
  167.2 2.8 copy.21
  170.0 3.2 pad_slice_fusion
  173.2 4.9 %copy.20 = bf16[7,128,1536]{2,1,0:T(8,128)(2,1)} copy(bf16[7,128,1536]{1,2,0:T(8,128)(2,1)} %get-tuple-element.7) | data formatting | bytes 5505024 | tf_op jit(solution)/shard_map/slice | solution.py:65
  183.7 6.5 %fusion.15 = f32[896,768]{1,0:T(8,128)} fusion(bf16[896,1536]{1,0:T(8,128)(2,1)} %bitcast.47, bf16[1536,3,768]{2,0,1:T(8,128)(2,1)} %all-gather.2.cloned.1.call-done), kind=kOutput, calls=%fused_computation.32 | convolution fusion | flops 2113929216 | bytes 7864320 | tf_op jit(solution)/shard_map/dot_general | solution.py:74
  190.2 130.5 %reduce-scatter.2.cloned.1.call-done = bf16[384,3,768]{2,0,1:T(8,128)(2,1)} async-done(((bf16[1536,3,768]{2,0,1:T(8,128)(2,1)}), bf16[384,3,768]{2,0,1:T(8,128)(2,1)}) %reduce-scatter.2.cloned.1.call-update) | async-done | bytes 1769488 | tf_op jit(solution)/shard_map/reduce_scatter | solution.py:92
  320.7 4.1 %fusion.14 = f32[896,768]{1,0:T(8,128)S(1)} fusion(bf16[896,1536]{1,0:T(8,128)(2,1)S(1)} %bitcast.45, bf16[1536,3,768]{2,0,1:T(8,128)(2,1)} %all-gather.2.cloned.1.call-done), kind=kOutput, calls=%fused_computation.30 | convolution fusion | flops 2113929216 | bytes 7864320 | tf_op jit(solution)/shard_map/dot_general | solution.py:74
  324.8 5.5 %add_add_fusion = f32[896,768]{1,0:T(8,128)} fusion(f32[896,768]{1,0:T(8,128)S(1)} %copy-done.11, f32[896,768]{1,0:T(8,128)S(1)} %fusion.14, bf16[896,1536]{1,0:T(8,128)(2,1)S(1)} %bitcast.46, bf16[1536,3,768]{2,0,1:T(8,128)(2,1)} %all-gather.2.cloned.1.call-done), kind=kOutput, calls=%fused_computation.26 | convolution fusion | flops 2115305472 | bytes 13369344 | tf_op jit(solution)/shard_map/dot_general | solution.py:74
  330.3 3.6 %copy.23 = f32[7,128,768]{1,2,0:T(8,128)} copy(f32[7,128,768]{2,1,0:T(8,128)} %bitcast.48) | data formatting | bytes 5505024 | tf_op jit(solution)/shard_map/reshape | solution.py:78
  333.9 3.2 fusion.9
  339.6 4.7 %all-reduce.4.cloned.1.call-done = bf16[384,3,768]{2,0,1:T(8,128)(2,1)} async-done(((bf16[384,3,768]{2,0,1:T(8,128)(2,1)}), bf16[384,3,768]{2,0,1:T(8,128)(2,1)}) %all-reduce.4.cloned.1.call-update) | async-done | bytes 1769488 | tf_op jit(solution)/shard_map/psum | solution.py:95
  344.3 3.6 %convert_element_type.38 = f32[384,3,768]{2,0,1:T(8,128)} convert(bf16[384,3,768]{2,0,1:T(8,128)(2,1)} %all-reduce.4.cloned.1.call-done) | non-fusion elementwise | flops 884736 | bytes 5308416 | tf_op jit(solution)/shard_map/convert_element_type | solution.py:95
  (45 shorter events, 16.2 us)
Async XLA Ops:
  7.2 176.5 %all-gather.2.cloned.1.call-start = ((), (), s32[]{:S(2)}) async-start(), calls=%async_computation.1 | async-start | bytes 8847360 | tf_op jit(solution)/shard_map/all_gather | solution.py:71
  7.9 312.7 %reduce-scatter.2.cloned.1.call-start = ((), (), s32[]{:S(2)}) async-start(), calls=%async_computation.2 | async-start | bytes 8847360 | tf_op jit(solution)/shard_map/reduce_scatter | solution.py:92
  8.6 7.8 %copy-start.9 = (s32[12]{0:T(128)S(1)}, s32[12]{0:T(128)}, u32[]{:S(2)}) copy-start(s32[12]{0:T(128)} %param.11) | copy-start | bytes 148
  12.8 9.8 %copy-start.10 = (pred[12]{0:T(512)(128)(4,1)S(1)}, pred[12]{0:T(512)(128)(4,1)}, u32[]{:S(2)}) copy-start(pred[12]{0:T(512)(128)(4,1)} %constant.29.clone.1) | copy-start | bytes 40
  12.8 50.4 %collective-permute-start = (bf16[6,128,768]{1,2,0:T(8,128)(2,1)}, bf16[6,128,768]{1,2,0:T(8,128)(2,1)S(1)}, u32[]{:S(2)}, u32[]{:S(2)}) collective-permute-start(bf16[6,128,768]{1,2,0:T(8,128)(2,1)} %constant_dynamic-slice_fusion.1), channel_id=1, source_target_pairs={{0,4},{4,8},{8,12},{12,0},{1,5},{5,9},{9,13},{13,1},{2,6},{6,10},{... | collective-permute-start | bytes 3538952 | tf_op jit(solution)/shard_map/ppermute | solution.py:12
  16.5 46.4 %collective-permute-start.1 = (bf16[6]{0:T(256)(128)(2,1)S(1)}, bf16[6]{0:T(256)(128)(2,1)S(1)}, u32[]{:S(2)}, u32[]{:S(2)}) collective-permute-start(bf16[6]{0:T(256)(128)(2,1)S(1)} %get-tuple-element.12), channel_id=1, source_target_pairs={{0,4},{4,8},{8,12},{12,0},{1,5},{5,9},{9,13},{13,1},{2,6},{6,10},{... | collective-permute-start | bytes 44 | tf_op jit(solution)/shard_map/ppermute | solution.py:12
  22.6 40.7 %copy-start.8 = (f32[768]{0:T(1024)S(1)}, f32[768]{0:T(1024)}, u32[]{:S(2)}) copy-start(f32[768]{0:T(1024)} %param.9) | copy-start | bytes 9220
  26.3 48.8 %copy-start = (bf16[12,128,768]{1,2,0:T(8,128)(2,1)S(1)}, bf16[12,128,768]{1,2,0:T(8,128)(2,1)}, u32[]{:S(2)}) copy-start(bf16[12,128,768]{1,2,0:T(8,128)(2,1)} %copy.24) | copy-start | bytes 7077892
  63.3 13.0 %copy-start.1 = (bf16[12,128,768]{1,2,0:T(8,128)(2,1)}, bf16[12,128,768]{1,2,0:T(8,128)(2,1)S(1)}, u32[]{:S(2)}) copy-start(bf16[12,128,768]{1,2,0:T(8,128)(2,1)S(1)} %constant_dynamic-update-slice_fusion.1) | copy-start | bytes 7077892
  73.4 76.1 %copy-start.4 = (bf16[7,128,768]{1,2,0:T(8,128)(2,1)}, bf16[7,128,768]{1,2,0:T(8,128)(2,1)S(1)}, u32[]{:S(2)}) copy-start(bf16[7,128,768]{1,2,0:T(8,128)(2,1)S(1)} %fusion.7) | copy-start | bytes 4128772
  73.4 76.1 %collective-permute-start.2 = (bf16[7,128,768]{1,2,0:T(8,128)(2,1)S(1)}, bf16[7,128,768]{1,2,0:T(8,128)(2,1)}, u32[]{:S(2)}, u32[]{:S(2)}) collective-permute-start(bf16[7,128,768]{1,2,0:T(8,128)(2,1)S(1)} %fusion.7), channel_id=1, source_target_pairs={{0,2},{2,0},{1,3},{3,1},{4,6},{6,4},{5,7},{7,5},{8,10},{10,8},{9,1... | collective-permute-start | bytes 4128776 | tf_op jit(solution)/shard_map/ppermute | solution.py:56
  76.3 72.1 %collective-permute-start.3 = (bf16[6,128,768]{1,2,0:T(8,128)(2,1)}, bf16[6,128,768]{1,2,0:T(8,128)(2,1)S(1)}, u32[]{:S(2)}, u32[]{:S(2)}) collective-permute-start(bf16[6,128,768]{1,2,0:T(8,128)(2,1)} %constant_dynamic-slice_fusion), channel_id=1, source_target_pairs={{0,4},{4,8},{8,12},{12,0},{1,5},{5,9},{9,13},{13,1},{2,6},{6,10},{... | collective-permute-start | bytes 3538952 | tf_op jit(solution)/shard_map/ppermute | solution.py:12
  149.5 5.2 %copy-start.7 = (bf16[12,128,768]{1,2,0:T(8,128)(2,1)S(1)}, bf16[12,128,768]{1,2,0:T(8,128)(2,1)}, u32[]{:S(2)}) copy-start(bf16[12,128,768]{1,2,0:T(8,128)(2,1)} %constant_dynamic-update-slice_fusion) | copy-start | bytes 7077892
  167.0 177.3 %all-reduce.4.cloned.1.call-start = ((), (), s32[]{:S(2)}) async-start(), calls=%async_computation.3 | async-start | bytes 3538944 | tf_op jit(solution)/shard_map/psum | solution.py:95
  173.2 4.9 %copy-start.3 = (bf16[7,128,1536]{1,2,0:T(8,128)(2,1)S(1)}, bf16[7,128,1536]{1,2,0:T(8,128)(2,1)}, u32[]{:S(2)}) copy-start(bf16[7,128,1536]{1,2,0:T(8,128)(2,1)} %get-tuple-element.6) | copy-start | bytes 8257540
  183.7 137.0 %copy-start.5 = (bf16[7,128,1536]{2,1,0:T(8,128)(2,1)S(1)}, bf16[7,128,1536]{2,1,0:T(8,128)(2,1)}, u32[]{:S(2)}) copy-start(bf16[7,128,1536]{2,1,0:T(8,128)(2,1)} %copy.21) | copy-start | bytes 8257540
  320.6 4.1 %copy-start.6 = (bf16[7,128,1536]{2,1,0:T(8,128)(2,1)S(1)}, bf16[7,128,1536]{2,1,0:T(8,128)(2,1)}, u32[]{:S(2)}) copy-start(bf16[7,128,1536]{2,1,0:T(8,128)(2,1)} %copy.22) | copy-start | bytes 8257540
  320.7 4.1 %copy-start.11 = (f32[896,768]{1,0:T(8,128)S(1)}, f32[896,768]{1,0:T(8,128)}, u32[]{:S(2)}) copy-start(f32[896,768]{1,0:T(8,128)} %fusion.15) | copy-start | bytes 8257540
  330.3 3.6 %copy-start.2 = (bf16[12,128,768]{1,2,0:T(8,128)(2,1)S(1)}, bf16[12,128,768]{1,2,0:T(8,128)(2,1)}, u32[]{:S(2)}) copy-start(bf16[12,128,768]{1,2,0:T(8,128)(2,1)} %copy-done.1) | copy-start | bytes 7077892
Sparse Core Ops, SparseCore 0:
  9.6 174.0 all-gather.1
  186.0 134.5 reduce-scatter.1
  323.0 21.2 all-reduce.3
